TPU v7x, 512 devices: a whole 4x4x16 slice. The times are simulated.
512 devices in a mesh: ctx: 16 (over z), exp: 32 (over y, x, core).
Axes of the slice: x: 4, y: 4, z: 16, core: 2. Of those that a mesh axis runs over, the one named last changes fastest.
Arguments:
- queries: bfloat16 [16384, 4096], P('ctx', 'exp'), may hold values from -6 to 6
- key_vectors: bfloat16 [16384, 4096], P('ctx', 'exp'), may hold values from -6 to 6
- value_vectors: bfloat16 [16384, 4096], P('ctx', 'exp'), may hold values from -6 to 6
- log_decay: float32 [16384, 32], P('ctx', 'exp'), may hold values from -2 to 0
- attn_gain: float32 [4096], P('exp'), may hold values from 0.1 to 1.9
- residual: bfloat16 [16384, 4096], P(('ctx', 'exp')), may hold values from -6 to 6
- expert_ids: int32 [16384, 1], P(('ctx', 'exp')), may hold values from 0 to 31; in each aligned block of 32 rows (0 to 31, 32 to 63, ...) at most 2 rows name the same one
- gate_weights: float32 [16384, 1], P(('ctx', 'exp')), may hold values from 0.5 to 1.5
- w_gate: bfloat16 [32, 4096, 768], P('exp', 'ctx'), may hold values from -0.09375 to 0.09375
- w_up: bfloat16 [32, 4096, 768], P('exp', 'ctx'), may hold values from -0.09375 to 0.09375
- w_down: bfloat16 [32, 768, 4096], P('exp', None, 'ctx'), may hold values from -0.21875 to 0.21875
Outputs:
- mixed: bfloat16 [16384, 4096], P(('ctx', 'exp'))
Inputs may be any that keep to these rules, and one draw needn't show every extreme that they name: `expert_ids`: within the rows of one device (aligned blocks of 32 rows) no expert is named more than 2 times.
All inputs are finite; a program needn't handle non-finite values.
Results may differ from a plain program's by a relative error of at most 0.03.
Values may be sent and summed in bfloat16 or wider, within the bound.
A program may use at most 64 MiB of HBM per device.

v0:
```python
from functools import partial

import jax
import jax.numpy as jnp
from jax import lax
from jax.sharding import PartitionSpec as P

HD = 128


PRECISE = lax.Precision.HIGHEST
EPSILON = 1e-06


def prefix(x, axis, join, neutral):
    place = lax.axis_index(axis)
    gathered = jax.tree.map(
        lambda a, kind: lax.all_gather(a.astype(kind), axis), x, (jnp.bfloat16, jnp.bfloat16)
    )
    state = jax.tree.map(lambda a, e: jnp.zeros_like(a) + jnp.asarray(e, a.dtype), x, neutral)

    def one(hop, state):
        return join(
            state,
            jax.tree.map(
                lambda a, own: lax.dynamic_index_in_dim(a, hop, 0, False).astype(own.dtype),
                gathered,
                x,
            ),
        )

    return lax.fori_loop(0, place, one, state)


def block_terms(query_rows, key_rows, value_rows, decay_rows, block_len):
    blocks = query_rows.shape[0] // block_len
    query_blocks = query_rows.reshape(blocks, block_len, -1)
    key_blocks = key_rows.reshape(blocks, block_len, -1)
    value_blocks = value_rows.reshape(blocks, block_len, -1)
    running = jnp.cumsum(decay_rows.reshape(blocks, block_len), axis=1)
    ending = running[:, -1]
    causal = jnp.arange(block_len)[:, None] >= jnp.arange(block_len)[None, :]
    scores = jnp.einsum(
        "bth,bsh->bts", query_blocks, key_blocks, preferred_element_type=jnp.float32
    )
    spread = jnp.where(causal[None], running[:, :, None] - running[:, None, :], -jnp.inf)
    weights = (scores * jnp.exp(spread)).astype(jnp.bfloat16)
    within = jnp.einsum("bts,bsh->bth", weights, value_blocks, preferred_element_type=jnp.float32)
    query_decayed = query_blocks.astype(jnp.float32) * jnp.exp(running)[:, :, None]
    key_decayed = key_blocks.astype(jnp.float32) * jnp.exp(ending[:, None] - running)[:, :, None]
    updates = jnp.einsum(
        "bsh,bsg->bhg", key_decayed, value_blocks.astype(jnp.float32), precision=PRECISE
    )
    carried = jnp.zeros(updates.shape[1:], jnp.float32)
    openings = []
    for block_index in range(blocks):
        openings.append(carried)
        carried = jnp.exp(ending[block_index]) * carried + updates[block_index]
    preceding = jnp.cumsum(ending) - ending
    return (within, query_decayed, jnp.stack(openings), preceding, carried, jnp.sum(ending))


def combine_states(earlier, following):
    return (
        earlier[0] + following[0],
        jnp.exp(following[0])[:, None, None] * earlier[1] + following[1],
    )


def shards(
    queries,
    key_vectors,
    value_vectors,
    log_decay,
    attn_gain,
    residual,
    expert_ids,
    gate_weights,
    w_gate,
    w_up,
    w_down,
):
    seclen, width_all = queries.shape
    heads_here = width_all // HD

    def split_heads(stacked):
        return stacked.reshape(seclen, heads_here, HD).transpose(1, 0, 2)

    block_len = min(512, seclen)
    within, query_decayed, openings, preceding, summary, section_total = jax.vmap(
        partial(block_terms, block_len=block_len)
    )(split_heads(queries), split_heads(key_vectors), split_heads(value_vectors), log_decay.T)
    identity = (jnp.zeros_like(section_total), jnp.zeros_like(summary))
    _, incoming = prefix((section_total, summary), "ctx", combine_states, identity)
    states = openings + jnp.exp(preceding)[:, :, None, None] * incoming[:, None]
    attention = within + jnp.einsum("kbth,kbhg->kbtg", query_decayed, states, precision=PRECISE)
    attention = attention.reshape(heads_here, seclen, HD)
    inverse_rms = lax.rsqrt(jnp.mean(attention * attention, axis=-1, keepdims=True) + EPSILON)
    normed = (attention * inverse_rms * attn_gain.reshape(heads_here, 1, HD)).astype(jnp.bfloat16)
    normed = normed.transpose(1, 0, 2).reshape(seclen, width_all)
    gathered = lax.all_to_all(normed, "exp", split_axis=0, concat_axis=1, tiled=True)
    hidden_in = (residual.astype(jnp.float32) + gathered.astype(jnp.float32)).astype(jnp.bfloat16)
    rows_here = hidden_in.shape[0]
    experts = lax.axis_size("exp") * w_gate.shape[0]
    capacity = max(2, 2 * rows_here // experts)
    chosen = expert_ids[:, 0]
    member = (chosen[:, None] == jnp.arange(experts)[None, :]).astype(jnp.int32)
    before_me = jnp.cumsum(member, axis=0) - member
    position = jnp.sum(before_me * member, axis=1)
    slot_index = chosen * capacity + position
    placing = (jnp.arange(experts * capacity)[:, None] == slot_index[None, :]).astype(jnp.bfloat16)
    outgoing = jnp.dot(placing, hidden_in, preferred_element_type=jnp.float32).astype(jnp.bfloat16)
    outgoing = outgoing.reshape(experts, capacity, -1)
    arrived = lax.all_to_all(
        lax.all_to_all(outgoing, "ctx", split_axis=2, concat_axis=1, tiled=True),
        "exp",
        split_axis=0,
        concat_axis=0,
        tiled=True,
    )
    feature_part = arrived.shape[2]
    expert_rows = arrived.reshape(-1, feature_part)
    gate_part = jnp.dot(expert_rows, w_gate[0], preferred_element_type=jnp.float32)
    up_part = jnp.dot(expert_rows, w_up[0], preferred_element_type=jnp.float32)
    summed = lax.psum_scatter(
        jnp.concatenate([gate_part, up_part], axis=1).astype(jnp.bfloat16),
        "ctx",
        scatter_dimension=0,
        tiled=True,
    ).astype(jnp.float32)
    width_ff = w_gate.shape[2]
    activated = (jax.nn.silu(summed[:, :width_ff]) * summed[:, width_ff:]).astype(jnp.bfloat16)
    expert_out = jnp.dot(
        activated,
        lax.all_gather(w_down, "ctx", axis=2, tiled=True)[0],
        preferred_element_type=jnp.float32,
    ).astype(jnp.bfloat16)
    groups = expert_out.shape[0] // (lax.axis_size("ctx") * capacity)
    shaped = expert_out.reshape(groups, lax.axis_size("ctx"), capacity, -1)
    returned = lax.all_to_all(
        lax.all_to_all(shaped, "ctx", split_axis=1, concat_axis=0, tiled=True),
        "exp",
        split_axis=0,
        concat_axis=0,
        tiled=True,
    )
    returned_rows = returned.reshape(experts * capacity, -1)
    combined = jnp.dot(placing.T, returned_rows, preferred_element_type=jnp.float32)
    mixed = hidden_in.astype(jnp.float32) + gate_weights * combined
    return mixed.astype(jnp.bfloat16)


def solution(mesh):
    return jax.shard_map(
        shards,
        mesh=mesh,
        in_specs=(
            P("ctx", "exp"),
            P("ctx", "exp"),
            P("ctx", "exp"),
            P("ctx", "exp"),
            P("exp"),
            P(("ctx", "exp"), None),
            P(("ctx", "exp"), None),
            P(("ctx", "exp"), None),
            P("exp", "ctx", None),
            P("exp", "ctx", None),
            P("exp", None, "ctx"),
        ),
        out_specs=P(("ctx", "exp"), None),
        check_vma=False,
    )
```

profile of v0, /device:TPU:1, one launch (start us, length us, event | category | flops | bytes accessed | tf_op | source)
XLA Modules:
  0.0 417.9 jit_solution(17059354903688054052)
XLA Ops:
  6.5 1.3 reduce-window.14
  7.9 0.2 slice_reduce_fusion
  8.0 0.1 copy.44
  8.2 0.2 reduce-window.18
  8.4 0.1 copy.32
  8.5 0.1 copy.43
  8.6 1.2 copy.35
  9.8 0.6 fusion.41
  10.4 0.7 fusion.43
  12.4 0.1 subtract_exponential_fusion
  12.5 1.3 convolution_bitcast_fusion
  13.8 31.8 %all_gather.15 = bf16[16,1,128,128]{3,2,1,0:T(8,128)(2,1)S(1)} all-gather(bf16[1,1,128,128]{3,2,1,0:T(8,128)(2,1)S(1)} %get-tuple-element.60), channel_id=1, replica_groups=mesh['ctx'=16,'exp'=32] {'ctx'}, dimensions={0}, use_global_device_ids=true | all-gather | bytes 557056 | tf_op jit(solution)/shard_map/all_gather | solution.py:18
  45.6 1.3 dynamic-slice
  47.0 1.4 dynamic-update-slice
  48.4 0.1 iota_compare_fusion
  48.5 20.5 %all-reduce.1 = bf16[16]{0:T(256)(128)(2,1)S(1)} all-reduce(bf16[16]{0:T(256)(128)(2,1)S(1)} %dynamic-update-slice), channel_id=1, replica_groups=mesh['ctx'=16,'exp'=32] {'ctx'}, use_global_device_ids=true, to_apply=%add.1 | all-reduce | flops 16 | bytes 64
  69.0 0.2 reduce-window.19
  69.2 0.7 fusion.16
  69.9 0.0 copy-done.7
  69.9 0.0 copy-done.8
  70.0 0.0 copy-start.11
  70.0 0.0 copy-start.9
  70.0 0.0 copy-start.3
  70.0 1.0 multiply_reduce_fusion
  71.0 0.1 rsqrt.12
  71.1 0.9 multiply_convert_fusion.1
  72.0 21.9 %all-to-all-start = ((bf16[32,32,128]{2,1,0:T(8,128)(2,1)}), bf16[32,32,128]{2,1,0:T(8,128)(2,1)S(1)}, u32[]{:S(2)}, u32[]{:S(2)}) async-start(bf16[32,32,128]{2,1,0:T(8,128)(2,1)} %multiply_convert_fusion.1), calls=%async_computation | async-start | bytes 524288 | tf_op jit(solution)/shard_map/all_to_all | solution.py:101
  93.9 0.0 reduce-scatter.4.cloned.1.call-start
  93.9 0.1 fusion.35
  94.0 0.1 reduce_window_sum.60
  94.1 0.2 select_reduce_fusion
  94.3 8.5 %all-to-all-done = bf16[32,32,128]{2,1,0:T(8,128)(2,1)S(1)} async-done(((bf16[32,32,128]{2,1,0:T(8,128)(2,1)}), bf16[32,32,128]{2,1,0:T(8,128)(2,1)S(1)}, u32[]{:S(2)}, u32[]{:S(2)}) %all-to-all-start) | async-done | bytes 262176 | tf_op jit(solution)/shard_map/all_to_all | solution.py:101
  102.8 0.3 convolution_convert_fusion
  103.1 0.4 copy-done.1
  103.5 0.3 reshape.345
  103.8 1.6 copy.37
  105.5 2.0 reshape.360
  107.4 43.4 %all_to_all.56 = bf16[16,2,8192]{2,1,0:T(2,128)(2,1)S(1)} all-to-all(bf16[16,2,8192]{2,1,0:T(2,128)(2,1)S(1)} %reshape.360), channel_id=1, replica_groups=mesh['ctx'=16,'exp'=32] {'ctx'}, dimensions={0} | all-to-all | bytes 1048576 | tf_op jit(solution)/shard_map/all_to_all | solution.py:115
  150.8 1.0 reshape.361
  151.9 1.1 copy.46
  153.0 0.0 copy-start.5
  153.0 0.3 copy.40
  153.3 21.8 %all_to_all.57 = bf16[32,32,256]{2,1,0:T(8,128)(2,1)S(1)} all-to-all(bf16[32,32,256]{2,1,0:T(8,128)(2,1)S(1)} %copy.40), channel_id=1, replica_groups=mesh['ctx'=16,'exp'=32] {'exp'}, dimensions={0} | all-to-all | bytes 1048576 | tf_op jit(solution)/shard_map/all_to_all | solution.py:114
  175.1 0.6 convolution_convert_fusion.1
  175.8 0.6 convolution_convert_fusion.2
  176.4 0.3 pad_maximum_fusion
  176.7 3.0 copy.47
  179.7 0.0 reduce-scatter.4.cloned.1.call-update
  179.8 0.0 all-gather.2.cloned.1.call-start
  179.8 0.7 all-gather.2.cloned.1.call-update
  180.5 58.9 %reduce-scatter.4.cloned.1.call-done = bf16[64,1536]{1,0:T(8,128)(2,1)} async-done(((bf16[1024,1536]{1,0:T(8,128)(2,1)}), bf16[64,1536]{1,0:T(8,128)(2,1)}) %reduce-scatter.4.cloned.1.call-update) | async-done | bytes 196624
  239.4 1.1 copy.48
  240.5 0.1 convert_element_type.106
  240.6 109.9 %all-gather.2.cloned.1.call-done = bf16[1,768,4096]{2,1,0:T(8,128)(2,1)} async-done(((bf16[1,768,256]{2,1,0:T(8,128)(2,1)}), bf16[1,768,4096]{2,1,0:T(8,128)(2,1)}) %all-gather.2.cloned.1.call-update) | async-done | bytes 6291472 | tf_op jit(solution)/shard_map/all_gather | solution.py:135
  350.5 4.1 fusion.2
  354.6 0.3 reshape.347
  354.9 0.0 copy-start.2
  354.9 0.0 copy-start.4
  354.9 0.0 copy-start.10
  354.9 0.5 copy.41
  355.4 23.5 %all_to_all.58 = bf16[2,16,2,4096]{3,2,0,1:T(2,128)(2,1)S(1)} all-to-all(bf16[2,16,2,4096]{3,2,0,1:T(2,128)(2,1)S(1)} %copy.41), channel_id=1, replica_groups=mesh['ctx'=16,'exp'=32] {'ctx'}, dimensions={1} | all-to-all | bytes 1048576 | tf_op jit(solution)/shard_map/all_to_all | solution.py:141
  378.9 30.9 %all_to_all.59 = bf16[32,1,2,4096]{3,2,1,0:T(2,128)(2,1)S(1)} all-to-all(bf16[32,1,2,4096]{3,2,1,0:T(2,128)(2,1)S(1)} %bitcast.99), channel_id=1, replica_groups=mesh['ctx'=16,'exp'=32] {'exp'}, dimensions={0} | all-to-all | bytes 1048576 | tf_op jit(solution)/shard_map/all_to_all | solution.py:140
  409.9 0.2 reshape.348
  410.1 1.0 fusion.6
  (24 shorter events, 0.1 us)
Async XLA Ops:
  6.5 168.6 %copy-start = (bf16[1,256,768]{2,1,0:T(8,128)(2,1)S(1)}, bf16[1,256,768]{2,1,0:T(8,128)(2,1)}, u32[]{:S(2)}) copy-start(bf16[1,256,768]{2,1,0:T(8,128)(2,1)} %param.22) | copy-start | bytes 1179652
  8.0 61.2 %copy-start.6 = (bf16[1024,128]{1,0:T(8,128)(2,1)S(1)}, bf16[1024,128]{1,0:T(8,128)(2,1)}, u32[]{:S(2)}) copy-start(bf16[1024,128]{1,0:T(8,128)(2,1)} %param.13) | copy-start | bytes 786436
  8.6 61.3 %copy-start.7 = (bf16[1024,128]{1,0:T(8,128)(2,1)S(1)}, bf16[1024,128]{1,0:T(8,128)(2,1)}, u32[]{:S(2)}) copy-start(bf16[1024,128]{1,0:T(8,128)(2,1)} %param.15) | copy-start | bytes 786436
  8.6 61.3 %copy-start.8 = (bf16[1024,128]{1,0:T(8,128)(2,1)S(1)}, bf16[1024,128]{1,0:T(8,128)(2,1)}, u32[]{:S(2)}) copy-start(bf16[1024,128]{1,0:T(8,128)(2,1)} %param.14) | copy-start | bytes 786436
  70.0 1.1 copy-start.11
  70.0 24.0 %copy-start.9 = (s32[32,1]{0,1:T(1,128)S(1)}, s32[32,1]{0,1:T(1,128)}, u32[]{:S(2)}) copy-start(s32[32,1]{0,1:T(1,128)} %param.19) | copy-start | bytes 388
  70.0 32.8 %copy-start.3 = (bf16[32,4096]{1,0:T(8,128)(2,1)S(1)}, bf16[32,4096]{1,0:T(8,128)(2,1)}, u32[]{:S(2)}) copy-start(bf16[32,4096]{1,0:T(8,128)(2,1)} %param.18) | copy-start | bytes 786436
  72.0 30.8 %all-to-all-start = ((bf16[32,32,128]{2,1,0:T(8,128)(2,1)}), bf16[32,32,128]{2,1,0:T(8,128)(2,1)S(1)}, u32[]{:S(2)}, u32[]{:S(2)}) async-start(bf16[32,32,128]{2,1,0:T(8,128)(2,1)} %multiply_convert_fusion.1), calls=%async_computation | async-start | bytes 524288 | tf_op jit(solution)/shard_map/all_to_all | solution.py:101
  93.9 145.5 %reduce-scatter.4.cloned.1.call-start = ((), (), s32[]{:S(2)}) async-start(), calls=%async_computation.7 | async-start | bytes 3342336
  102.8 0.7 copy-start.1
  153.0 22.8 %copy-start.5 = (bf16[1,256,768]{2,1,0:T(8,128)(2,1)S(1)}, bf16[1,256,768]{2,1,0:T(8,128)(2,1)}, u32[]{:S(2)}) copy-start(bf16[1,256,768]{2,1,0:T(8,128)(2,1)} %param.21) | copy-start | bytes 1179652
  179.8 170.7 %all-gather.2.cloned.1.call-start = ((), (), s32[]{:S(2)}) async-start(), calls=%async_computation.6 | async-start | bytes 6684672 | tf_op jit(solution)/shard_map/all_gather | solution.py:135
  354.9 55.2 %copy-start.2 = (bf16[32,32,128]{2,1,0:T(8,128)(2,1)S(1)}, bf16[32,32,128]{2,1,0:T(8,128)(2,1)}, u32[]{:S(2)}) copy-start(bf16[32,32,128]{2,1,0:T(8,128)(2,1)} %copy-done.1) | copy-start | bytes 786436
  354.9 55.2 %copy-start.4 = (bf16[32,4096]{1,0:T(8,128)(2,1)S(1)}, bf16[32,4096]{1,0:T(8,128)(2,1)}, u32[]{:S(2)}) copy-start(bf16[32,4096]{1,0:T(8,128)(2,1)} %param.18) | copy-start | bytes 786436
  354.9 55.2 %copy-start.10 = (f32[32,1]{0,1:T(1,128)S(1)}, f32[32,1]{0,1:T(1,128)}, u32[]{:S(2)}) copy-start(f32[32,1]{0,1:T(1,128)} %param.20) | copy-start | bytes 388
Sparse Core Ops, SparseCore 0:
  179.9 59.4 reduce-scatter.3
  241.4 109.0 all-gather.1
where the time goes:
time: 420 us; the launch traced here: 418 us
  waiting for transfers between devices  178 us (42%)
  blocking collectives  172 us (41%)
  starting transfers between devices  21.9 us (5%)
  local copies, waits for them, and re-layouts  17.2 us (4%)
  between operations  15.1 us (4%)
  matrix products  9.6 us (2%)
    all_gather x1, waiting for transfers between devices, shards(): lax.all_gather(w_down, 'ctx', axis=2, tiled=True)[0]  110 us
    unnamed x3, waiting for transfers between devices  59.6 us
    all_to_all x1, blocking collectives, shards(): lax.all_to_all(outgoing, 'ctx', split_axis=2, concat_axis=1, tiled=True)  43.4 us
    all_gather x1, blocking collectives, prefix(): lax.all_gather(a.astype(kind), axis)  31.8 us
    all_to_all x1, blocking collectives, shards(): lax.all_to_all(lax.all_to_all(shaped, 'ctx', split_axis=1, concat_axis=0,...  30.9 us
    all_to_all x1, blocking collectives, shards(): lax.all_to_all(shaped, 'ctx', split_axis=1, concat_axis=0, tiled=True)  23.5 us
    all_to_all x1, starting transfers between devices, shards(): lax.all_to_all(normed, 'exp', split_axis=0, concat_axis=1, tiled=True)  21.9 us
    all_to_all x1, blocking collectives, shards(): lax.all_to_all(lax.all_to_all(outgoing, 'ctx', split_axis=2, concat_axis=...  21.8 us
  transfers between devices with their start and end apart: 3, of which 3 were waited for; matrix products, arithmetic and copies ran while one was open for 0% of the time, Pallas kernels for 0%

commit v1 on v0

v1 whole, which is shorter than its diff:
```python
import functools

import jax
import jax.numpy as jnp
from jax import lax
from jax.experimental import pallas as pl
from jax.experimental.pallas import tpu as pltpu
from jax.sharding import PartitionSpec as P

MESH = pl.DeviceIdType.MESH
F32, BF16 = jnp.float32, jnp.bfloat16
PRECISE = lax.Precision.HIGHEST
EPSILON = 1e-06
NZ, NE = 16, 32
HD, BL, SEC, ROWS, DS, FFE = 128, 512, 1024, 32, 256, 768
TILES = SEC // 128
CHUNK = 64
HALF = NZ // 2
SUBS = 4
WIDE = 2 * FFE // SUBS


def dot(a, b, **kw):
    return jnp.dot(a, b, preferred_element_type=F32, **kw)


def dot_t(a, b):
    return lax.dot_general(a, b, (((1,), (1,)), ((), ())), preferred_element_type=F32)


def t_dot(a, b):
    return lax.dot_general(a, b, (((0,), (0,)), ((), ())), preferred_element_type=F32)


def iota(shape, dim):
    return lax.broadcasted_iota(jnp.int32, shape, dim)


def kernel(
    q_ref, k_ref, v_ref, decay_ref, gain_ref, res_ref, ids_ref, gw_ref, wg_ref, wu_ref, wd_ref,
    out_ref,
    info, coef, group, quarter, prefix, within, normed, heads, hidden, zrows, place, slots, erows,
    send_r, recv_r, send_l, recv_l, act, produced, fromexp, yrows, yback,
    s_info, r_info, s_grp, r_grp, s_qtr, r_qtr, s_pre, r_pre, s_hd, r_hd, s_zr, r_zr, s_sl, r_sl,
    s_rr, r_rr, s_rl, r_rl, s_ar, r_ar, s_al, r_al, s_pr, r_pr, s_yb, r_yb,
):
    z, e = lax.axis_index("ctx"), lax.axis_index("exp")
    right, left = lax.rem(z + 1, NZ), lax.rem(z + NZ - 1, NZ)
    member, base = lax.rem(z, 4), z - lax.rem(z, 4)
    grp = z // 4

    def remote(src, dst, ss, rs, to_z, to_e):
        return pltpu.make_async_remote_copy(
            src_ref=src, dst_ref=dst, send_sem=ss, recv_sem=rs,
            device_id=(to_z, to_e), device_id_type=MESH,
        )

    def loop(lo, hi, body):
        def step(i, c):
            body(i)
            return c
        lax.fori_loop(lo, hi, step, 0)

    barrier = pltpu.get_barrier_semaphore()
    loop(1, NZ, lambda i: pl.semaphore_signal(
        barrier, inc=1, device_id=(lax.rem(z + i, NZ), e), device_id_type=MESH))
    loop(1, NE, lambda i: pl.semaphore_signal(
        barrier, inc=1, device_id=(z, lax.rem(e + i, NE)), device_id_type=MESH))

    lane, sub = iota((ROWS, 128), 1), iota((ROWS, 128), 0)
    eye = iota((ROWS, ROWS), 1) == iota((ROWS, ROWS), 0)
    ids_col = jnp.sum(jnp.where(eye, ids_ref[...].astype(F32), 0.0), axis=1, keepdims=True)
    near = lax.rem(lane, ROWS)
    ids_row = jnp.sum(jnp.where(sub == near, ids_col, 0.0), axis=0, keepdims=True)
    same = jnp.where((ids_col == ids_row) & (sub < near), 1.0, 0.0)
    slot_row = ids_row * 32.0 + jnp.sum(same, axis=0, keepdims=True)

    decay = jnp.concatenate([decay_ref[:, 128 * r:128 * r + 128] for r in range(TILES)], axis=0)
    upto = jnp.where(iota((128, 128), 0) <= iota((128, 128), 1), 1.0, 0.0)
    cum = dot(decay, upto, precision=PRECISE)
    tail = jnp.broadcast_to(cum[:, 127:128], (TILES, 128))
    r_to, r_from = iota((TILES, TILES), 0), iota((TILES, TILES), 1)
    earlier = jnp.where((r_from < r_to) & (r_from // 4 == r_to // 4), 1.0, 0.0)
    running = cum + dot(earlier, tail, precision=PRECISE)
    running_col = running.T
    ends = [running[4 * b + 3:4 * b + 4, 127:128] for b in range(2)]
    total = ends[0] + ends[1]

    updates = []
    for b in range(2):
        rest = jnp.concatenate(
            [jnp.exp(ends[b] - running_col[:, 4 * b + r:4 * b + r + 1]) for r in range(4)], axis=0
        )
        decayed = (v_ref[BL * b:BL * b + BL, :].astype(F32) * rest).astype(BF16)
        updates.append(t_dot(k_ref[BL * b:BL * b + BL, :], decayed))
    own_state = jnp.exp(ends[1]) * updates[0] + updates[1]

    quart = iota((1, 128), 1) // 32
    info[z] = jnp.where(quart == member, slot_row, 0.0) + jnp.where(
        quart == lax.rem(z + 1, 4), total, 0.0
    )
    group[member] = own_state.astype(BF16)
    pl.semaphore_wait(barrier, NZ - 1 + NE - 1)

    def cp_info(i):
        return remote(info.at[z], info.at[z], s_info.at[i], r_info.at[i], lax.rem(z + i, NZ), e)

    def cp_group(i):
        return remote(group.at[member], group.at[member], s_grp.at[i], r_grp.at[i],
                      base + lax.rem(member + i, 4), e)

    def cp_quarter(i):
        return remote(quarter.at[grp], quarter.at[grp], s_qtr.at[i], r_qtr.at[i],
                      lax.rem(z + 4 * i, NZ), e)

    def cp_prefix(i):
        return remote(prefix.at[member], prefix.at[member], s_pre.at[i], r_pre.at[i],
                      base + lax.rem(member + i, 4), e)

    loop(1, NZ, lambda i: cp_info(i).start())
    loop(1, 4, lambda i: cp_group(i).start())

    for b in range(2):
        for i in range(4):
            r, width = 4 * b + i, 128 * (i + 1)
            rows = pl.ds(128 * r, 128)
            span = pl.ds(BL * b, width)
            scores = dot_t(q_ref[rows, :], k_ref[span, :])
            col = running_col[:, r:r + 1]
            weights = []
            for j in range(i + 1):
                spread = col - running[4 * b + j:4 * b + j + 1, :]
                if j == i:
                    spread = jnp.where(iota((128, 128), 0) >= iota((128, 128), 1), spread, -jnp.inf)
                weights.append((scores[:, 128 * j:128 * j + 128] * jnp.exp(spread)).astype(BF16))
            weights = jnp.concatenate(weights, axis=1) if i else weights[0]
            within[rows, :] = dot(weights, v_ref[span, :])

    loop(1, NZ, lambda i: cp_info(i).wait_recv())
    table = info[:, 0, :]
    zrow, zlane = iota((NZ, 128), 0), iota((NZ, 128), 1)
    totals = jnp.sum(jnp.where(zlane == 32 * lax.rem(zrow + 1, 4), table, 0.0), axis=1, keepdims=True)
    totals = jnp.broadcast_to(totals, (NZ, 128))
    src, mid = iota((NZ, NZ), 0), iota((NZ, NZ), 1)

    def decays(mask, keep):
        between = dot(jnp.where(mask, 1.0, 0.0), totals, precision=PRECISE)
        return jnp.where(keep, jnp.exp(between), 0.0)

    coef[0] = decays((mid > src) & (mid < base + 4), zrow >= 0)
    coef[1] = decays((mid >= 4 * src + 4) & (mid < base), zrow < grp)
    coef[2] = decays((mid > src) & (mid < z), zrow < z)
    coef[3] = decays((mid >= base) & (mid < z), zrow >= 0)

    loop(1, 4, lambda i: cp_group(i).wait_recv())
    part = pl.ds(pl.multiple_of(member * 32, 32), 32)
    whole = jnp.zeros((32, HD), F32)
    for m in range(4):
        whole += coef[0, pl.ds(base + m, 1), :] * group[m, part, :].astype(F32)
    quarter[grp] = whole.astype(BF16)
    loop(1, 4, lambda i: cp_quarter(i).start())
    loop(1, 4, lambda i: cp_quarter(i).wait_recv())
    before = jnp.zeros((32, HD), F32)
    for m in range(4):
        before += coef[1, m:m + 1, :] * quarter[m].astype(F32)
    prefix[member] = before.astype(BF16)
    loop(1, 4, lambda i: cp_prefix(i).start())
    incoming = jnp.zeros((HD, HD), F32)
    for m in range(4):
        incoming += coef[2, pl.ds(base + m, 1), :] * group[m].astype(F32)
    loop(1, 4, lambda i: cp_prefix(i).wait_recv())
    incoming += coef[3, 0:1, :] * prefix[...].reshape(HD, HD).astype(F32)

    gain = gain_ref[...]
    for b in range(2):
        state = incoming if b == 0 else updates[0] + jnp.exp(ends[0]) * incoming
        state = state.astype(BF16)
        for i in range(4):
            r = 4 * b + i
            rows = pl.ds(128 * r, 128)
            across = dot(q_ref[rows, :], state) * jnp.exp(running_col[:, r:r + 1])
            attention = within[rows, :] + across
            scale = lax.rsqrt(jnp.mean(attention * attention, axis=1, keepdims=True) + EPSILON)
            normed[rows, :] = (attention * scale * gain).astype(BF16)

    def cp_heads(i):
        to = lax.rem(e + i, NE)
        return remote(normed.at[pl.ds(pl.multiple_of(to * ROWS, ROWS), ROWS)], heads.at[e],
                      s_hd.at[i], r_hd.at[i], z, to)

    loop(1, NE, lambda i: cp_heads(i).start())
    heads[e] = normed[pl.ds(pl.multiple_of(e * ROWS, ROWS), ROWS), :]

    picks = []
    for g in range(4):
        mine = (zlane // 32 == lax.rem(zrow, 4)) & (zrow // 4 == g)
        row = jnp.sum(jnp.where(mine, table + 2.0 * zrow.astype(F32), 0.0), axis=0, keepdims=True)
        picks.append(row)
    picks = jnp.concatenate(picks, axis=1).astype(jnp.int32)
    for t in range(8):
        place[128 * t:128 * t + 128, :] = jnp.where(
            iota((128, NZ * ROWS), 0) + 128 * t == picks, 1.0, 0.0
        ).astype(BF16)

    loop(1, NE, lambda i: cp_heads(i).wait_recv())
    for c in range(NZ):
        both = jnp.concatenate([heads[2 * c], heads[2 * c + 1]], axis=1).astype(F32)
        hidden[c] = (res_ref[:, DS * c:DS * c + DS].astype(F32) + both).astype(BF16)

    def cp_rows(i):
        to = lax.rem(z + i, NZ)
        return remote(hidden.at[to], zrows.at[z], s_zr.at[i], r_zr.at[i], to, e)

    loop(1, NZ, lambda i: cp_rows(i).start())
    zrows[z] = hidden[z]
    loop(1, NZ, lambda i: cp_rows(i).wait_recv())
    slots[...] = dot(place[...], zrows[...].reshape(NZ * ROWS, DS)).astype(BF16)

    def cp_slots(i):
        to = lax.rem(e + i, NE)
        return remote(slots.at[pl.ds(pl.multiple_of(to * 32, 32), 32)], erows.at[e],
                      s_sl.at[i], r_sl.at[i], z, to)

    loop(1, NE, lambda i: cp_slots(i).start())
    erows[e] = slots[pl.ds(pl.multiple_of(e * 32, 32), 32), :]
    loop(1, NE, lambda i: cp_slots(i).wait_recv())

    def columns(u):
        side, off = divmod(u * WIDE, FFE)
        return (wg_ref, wu_ref)[side][:, off:off + WIDE]

    def own(dest, u):
        rows = erows[pl.ds(2 * dest, 2)].reshape(CHUNK, DS)
        return dot(rows, columns(u))

    def cp_right(s, u):
        return remote(send_r.at[s, u], recv_r.at[s, u], s_rr.at[s, u], r_rr.at[s, u], right, e)

    def cp_left(s, u):
        return remote(send_l.at[s, u], recv_l.at[s, u], s_rl.at[s, u], r_rl.at[s, u], left, e)

    for s in range(HALF):
        to_r = lax.rem(z + HALF - s, NZ)
        to_l = lax.rem(z + HALF + 1 + s, NZ)
        for u in range(SUBS):
            mine = own(to_r, u)
            if s:
                cp_right(s - 1, u).wait_recv()
                mine += recv_r[s - 1, u].astype(F32)
            send_r[s, u] = mine.astype(BF16)
            cp_right(s, u).start()
            if s < HALF - 1:
                mine = own(to_l, u)
                if s:
                    cp_left(s - 1, u).wait_recv()
                    mine += recv_l[s - 1, u].astype(F32)
                send_l[s, u] = mine.astype(BF16)
                cp_left(s, u).start()
    sums = []
    for u in range(SUBS):
        mine = own(z, u)
        cp_left(HALF - 2, u).wait_recv()
        mine += recv_l[HALF - 2, u].astype(F32)
        cp_right(HALF - 1, u).wait_recv()
        sums.append(mine + recv_r[HALF - 1, u].astype(F32))
    for u in range(SUBS // 2):
        gate, up = sums[u], sums[u + SUBS // 2]
        act[z, :, WIDE * u:WIDE * u + WIDE] = (gate / (1.0 + jnp.exp(-gate)) * up).astype(BF16)

    def cp_act_r(s, u):
        at = act.at[lax.rem(z + NZ - s, NZ), pl.ds(32 * u, 32)]
        return remote(at, at, s_ar.at[s, u], r_ar.at[s, u], right, e)

    def cp_act_l(s, u):
        at = act.at[lax.rem(z + s, NZ), pl.ds(32 * u, 32)]
        return remote(at, at, s_al.at[s, u], r_al.at[s, u], left, e)

    def cp_produced(d):
        return remote(produced.at[d], fromexp.at[e], s_pr.at[d], r_pr.at[e], z, d)

    def down(chunk):
        rows = dot(act[chunk], wd_ref[...]).astype(BF16)
        for u in range(2):
            d = 2 * chunk + u
            produced[d] = rows[32 * u:32 * u + 32]

            @pl.when(d != e)
            def _():
                cp_produced(d).start()

            @pl.when(d == e)
            def _():
                fromexp[e] = produced[d]

    for u in range(2):
        cp_act_r(0, u).start()
        cp_act_l(0, u).start()
    down(z)
    for s in range(HALF):
        for u in range(2):
            cp_act_r(s, u).wait_recv()
            if s < HALF - 1:
                cp_act_r(s + 1, u).start()
            if s < HALF - 1:
                cp_act_l(s, u).wait_recv()
                if s < HALF - 2:
                    cp_act_l(s + 1, u).start()
        down(lax.rem(z + NZ - 1 - s, NZ))
        if s < HALF - 1:
            down(lax.rem(z + 1 + s, NZ))

    def cp_from(i):
        src_e = lax.rem(e + i, NE)
        return remote(produced.at[src_e], fromexp.at[src_e], s_pr.at[src_e], r_pr.at[src_e], z, src_e)

    loop(1, NE, lambda i: cp_from(i).wait_recv())
    back = t_dot(place[...], fromexp[...].reshape(NE * 32, DS)).astype(BF16)
    yrows[...] = back.reshape(NZ, ROWS, DS)

    def cp_back(i):
        to = lax.rem(z + i, NZ)
        return remote(yrows.at[to], yback.at[z], s_yb.at[i], r_yb.at[i], to, e)

    loop(1, NZ, lambda i: cp_back(i).start())
    yback[z] = yrows[z]
    gw_col = jnp.sum(jnp.where(eye, gw_ref[...], 0.0), axis=1, keepdims=True)
    loop(1, NZ, lambda i: cp_back(i).wait_recv())
    for c in range(NZ):
        mixed = hidden[c].astype(F32) + gw_col * yback[c].astype(F32)
        out_ref[:, DS * c:DS * c + DS] = mixed.astype(BF16)

    loop(1, NZ, lambda i: cp_info(i).wait_send())
    loop(1, 4, lambda i: cp_group(i).wait_send())
    loop(1, 4, lambda i: cp_quarter(i).wait_send())
    loop(1, 4, lambda i: cp_prefix(i).wait_send())
    loop(1, NE, lambda i: cp_heads(i).wait_send())
    loop(1, NZ, lambda i: cp_rows(i).wait_send())
    loop(1, NE, lambda i: cp_slots(i).wait_send())
    for u in range(SUBS):
        for s in range(HALF):
            cp_right(s, u).wait_send()
            if s < HALF - 1:
                cp_left(s, u).wait_send()
    for u in range(2):
        for s in range(HALF):
            cp_act_r(s, u).wait_send()
            if s < HALF - 1:
                cp_act_l(s, u).wait_send()
    loop(1, NE, lambda i: cp_from(i).wait_send())
    loop(1, NZ, lambda i: cp_back(i).wait_send())


def shards(q, k, v, log_decay, gain, residual, ids, gate_weights, w_gate, w_up, w_down):
    sem = pltpu.SemaphoreType.DMA
    pair = lambda *shape: [sem(shape), sem(shape)]
    scratch = [
        pltpu.VMEM((NZ, 1, 128), F32),
        pltpu.VMEM((4, NZ, 128), F32),
        pltpu.VMEM((4, HD, HD), BF16),
        pltpu.VMEM((4, 32, HD), BF16),
        pltpu.VMEM((4, 32, HD), BF16),
        pltpu.VMEM((SEC, HD), F32),
        pltpu.VMEM((SEC, HD), BF16),
        pltpu.VMEM((NE, ROWS, HD), BF16),
        pltpu.VMEM((NZ, ROWS, DS), BF16),
        pltpu.VMEM((NZ, ROWS, DS), BF16),
        pltpu.VMEM((NE * 32, NZ * ROWS), BF16),
        pltpu.VMEM((NE * 32, DS), BF16),
        pltpu.VMEM((NE, 32, DS), BF16),
        pltpu.VMEM((HALF, SUBS, CHUNK, WIDE), BF16),
        pltpu.VMEM((HALF, SUBS, CHUNK, WIDE), BF16),
        pltpu.VMEM((HALF, SUBS, CHUNK, WIDE), BF16),
        pltpu.VMEM((HALF, SUBS, CHUNK, WIDE), BF16),
        pltpu.VMEM((NZ, CHUNK, FFE), BF16),
        pltpu.VMEM((NE, 32, DS), BF16),
        pltpu.VMEM((NE, 32, DS), BF16),
        pltpu.VMEM((NZ, ROWS, DS), BF16),
        pltpu.VMEM((NZ, ROWS, DS), BF16),
        *pair(NZ), *pair(4), *pair(4), *pair(4), *pair(NE), *pair(NZ), *pair(NE),
        *pair(HALF, SUBS), *pair(HALF, SUBS), *pair(HALF, 2), *pair(HALF, 2), *pair(NE), *pair(NZ),
    ]
    vmem = pl.BlockSpec(memory_space=pltpu.VMEM)
    return pl.pallas_call(
        kernel,
        out_shape=jax.ShapeDtypeStruct(residual.shape, BF16),
        in_specs=[vmem] * 11,
        out_specs=vmem,
        scratch_shapes=scratch,
        name="layer_pair",
        compiler_params=pltpu.CompilerParams(
            collective_id=0, has_side_effects=True, vmem_limit_bytes=48 << 20
        ),
    )(
        q, k, v, log_decay.T, gain.reshape(1, HD), residual, ids.T, gate_weights.T,
        w_gate[0], w_up[0], w_down[0],
    )


def solution(mesh):
    return jax.shard_map(
        shards,
        mesh=mesh,
        in_specs=(
            P("ctx", "exp"),
            P("ctx", "exp"),
            P("ctx", "exp"),
            P("ctx", "exp"),
            P("exp"),
            P(("ctx", "exp"), None),
            P(("ctx", "exp"), None),
            P(("ctx", "exp"), None),
            P("exp", "ctx", None),
            P("exp", "ctx", None),
            P("exp", None, "ctx"),
        ),
        out_specs=P(("ctx", "exp"), None),
        check_vma=False,
    )
```

time: 420 us -> 166 us (0.40)
  waiting for transfers between devices: 178 us -> 0 us
  blocking collectives: 172 us -> 0 us
  Pallas kernels: 0 us -> 158 us
  starting transfers between devices: 21.9 us -> 0 us
  between operations: 15.1 us -> 0.03 us
  matrix products: 9.6 us -> 0 us
  local copies, waits for them, and re-layouts: 17.2 us -> 8.18 us
    pallas_call x0 -> x1, Pallas kernels: none -> 158 us  [shards(): pl.pallas_call(kernel, out_shape=jax.ShapeDtypeStruct(residual.shape, BF1...]
    all_to_all x4 -> x0, blocking collectives: 120 us -> none  [the longest x1 43.4 us: shards(): lax.all_to_all(outgoing, 'ctx', split_axis=2, concat_axis=1, tiled=True)]
    all_gather x1 -> x0, waiting for transfers between devices: 110 us -> none  [shards(): lax.all_gather(w_down, 'ctx', axis=2, tiled=True)[0]]
    unnamed x3 -> x0, waiting for transfers between devices: 59.6 us -> none
    all_gather x1 -> x0, blocking collectives: 31.8 us -> none  [prefix(): lax.all_gather(a.astype(kind), axis)]
    all_to_all x1 -> x0, starting transfers between devices: 21.9 us -> none  [shards(): lax.all_to_all(normed, 'exp', split_axis=0, concat_axis=1, tiled=True)]
    unnamed x1 -> x0, blocking collectives: 20.5 us -> none
    dot_general x8 -> x0, matrix products: 9.6 us -> none  [the longest x1 4.05 us: shards(): jnp.dot(activated, lax.all_gather(w_down, 'ctx', axis=2, tiled=True)[0],...]
  transfers between devices with their start and end apart: 3 -> 0, of which waited for: 3 -> 0; matrix products, arithmetic and copies ran while one was open for 0% -> 0% of each run, Pallas kernels for 0% -> 0%
where the time goes in v1:
time: 166 us
  Pallas kernels  158 us (95%)
  local copies, waits for them, and re-layouts  8.18 us (5%)
    pallas_call x1, Pallas kernels, shards(): pl.pallas_call(kernel, out_shape=jax.ShapeDtypeStruct(residual.shape, BF1...  158 us
    unnamed x23, local copies, waits for them, and re-layouts  8.18 us

profile of v1, /device:TPU:1, one launch (start us, length us, event | category | flops | bytes accessed | tf_op | source)
XLA Modules:
  0.0 165.9 jit_solution(12144786879254241962)
XLA Ops:
  0.0 0.0 copy-start.7
  0.0 0.0 copy-start.8
  0.0 0.0 copy-start.9
  0.0 0.0 copy-start.10
  0.0 0.7 copy-done.7
  0.7 0.0 copy-done.8
  0.7 0.0 copy-done.9
  0.7 0.0 copy-done.10
  0.7 0.0 copy-start
  0.7 1.0 copy-done
  1.7 0.0 copy-start.1
  1.7 1.0 copy-done.1
  2.7 0.0 copy-start.2
  2.7 1.0 copy-done.2
  3.7 0.0 copy-start.3
  3.7 0.9 copy-done.3
  4.6 0.0 copy-start.4
  4.6 0.9 copy-done.4
  5.6 0.0 copy-start.5
  5.6 0.9 copy-done.5
  6.5 0.0 copy-start.6
  6.5 0.9 copy-done.6
  7.5 157.6 %layer_pair.1 = bf16[32,4096]{1,0:T(8,128)(2,1)S(1)} custom-call(bf16[1024,128]{1,0:T(8,128)(2,1)S(1)} %copy-done.3, bf16[1024,128]{1,0:T(8,128)(2,1)S(1)} %copy-done.4, bf16[1024,128]{1,0:T(8,128)(2,1)S(1)} %copy-done.5, f32[1,1024]{1,0:T(1,128)S(1)} %bitcast.10, f32[1,128]{1,0:T(1,128)S(1)} %bitcast.11, bf16[32,4096]{1,0:T(8,128)(2,1)S(1)} %copy-done.6, ...), custom_call_target="tpu_custom_call" | custom-call | tf_op jit(solution)/shard_map/layer_pair/pallas_call | solution.py:383
  165.1 0.7 copy.13
Async XLA Ops:
  0.0 0.7 copy-start.7
  0.0 0.7 copy-start.8
  0.0 0.7 copy-start.9
  0.0 0.7 copy-start.10
  0.7 1.0 copy-start
  1.7 1.0 copy-start.1
  2.7 1.0 copy-start.2
  3.7 0.9 copy-start.3
  4.6 0.9 copy-start.4
  5.6 0.9 copy-start.5
  6.5 0.9 copy-start.6

commit v2 on v1

v2 whole, which is shorter than its diff:
```python
import functools

import jax
import jax.numpy as jnp
from jax import lax
from jax.experimental import pallas as pl
from jax.experimental.pallas import tpu as pltpu
from jax.sharding import PartitionSpec as P

MESH = pl.DeviceIdType.MESH
F32, BF16 = jnp.float32, jnp.bfloat16
PRECISE = lax.Precision.HIGHEST
EPSILON = 1e-06
NZ, NE = 16, 32
HD, BL, SEC, ROWS, DS, FFE = 128, 512, 1024, 32, 256, 768
TILES = SEC // 128
CHUNK = 64
HALF = NZ // 2
SUBS = 4
FAR = sorted(range(1, NZ), key=lambda i: (-min(i, NZ - i), i))
WIDE = 2 * FFE // SUBS


def dot(a, b, **kw):
    return jnp.dot(a, b, preferred_element_type=F32, **kw)


def dot_t(a, b):
    return lax.dot_general(a, b, (((1,), (1,)), ((), ())), preferred_element_type=F32)


def t_dot(a, b):
    return lax.dot_general(a, b, (((0,), (0,)), ((), ())), preferred_element_type=F32)


def iota(shape, dim):
    return lax.broadcasted_iota(jnp.int32, shape, dim)


def kernel(
    q_hbm, k_hbm, v_hbm, decay_hbm, gain_hbm, res_hbm, ids_hbm, gw_hbm, wg_hbm, wu_hbm, wd_hbm,
    out_ref,
    q_ref, k_ref, v_ref, decay_ref, gain_ref, res_ref, ids_ref, gw_ref, wg_ref, wu_ref, wd_ref,
    info, pieces, gathered, entering, incoming, within, normed, heads, hidden, zrows, place, unplace,
    slots, erows, own_r, own_l, send_r, recv_r, send_l, recv_l, act, produced, fromexp, yrows, yback,
    s_in, s_wd, r_wd, s_info, r_info, s_pc, r_pc, s_en, r_en, s_hd, r_hd, s_zr, r_zr, s_sl, r_sl,
    s_rr, r_rr, s_rl, r_rl, s_ac, r_ac, s_pr, r_pr, s_yb, r_yb,
):
    z, e = lax.axis_index("ctx"), lax.axis_index("exp")
    right, left = lax.rem(z + 1, NZ), lax.rem(z + NZ - 1, NZ)
    chip = e // 2
    half, parity = z // 8, lax.rem(z, 2)
    partner = z + 1 - 2 * parity

    def remote(src, dst, ss, rs, to_z, to_e):
        return pltpu.make_async_remote_copy(
            src_ref=src, dst_ref=dst, send_sem=ss, recv_sem=rs,
            device_id=(to_z, to_e), device_id_type=MESH,
        )

    def loop(lo, hi, body):
        def step(i, c):
            body(i)
            return c
        lax.fori_loop(lo, hi, step, 0)

    drains = []

    def finish():
        for d in drains:
            d()
        drains.clear()

    staged = {}
    for n, (src, dst) in enumerate((
        (decay_hbm, decay_ref), (ids_hbm, ids_ref), (k_hbm, k_ref), (v_hbm, v_ref), (q_hbm, q_ref),
        (gain_hbm, gain_ref), (res_hbm, res_ref), (wg_hbm, wg_ref), (wu_hbm, wu_ref),
        (wd_hbm, wd_ref.at[parity]), (gw_hbm, gw_ref),
    )):
        copy = pltpu.make_async_copy(src, dst, s_in.at[n])
        staged[id(wd_ref) if src is wd_hbm else id(dst)] = copy
        copy.start()

    def need(*refs):
        for ref in refs:
            staged.pop(id(ref)).wait()

    barrier = pltpu.get_barrier_semaphore()
    for i in FAR:
        pl.semaphore_signal(
            barrier, inc=1, device_id=(lax.rem(z + i, NZ), e), device_id_type=MESH)
    loop(1, NE, lambda i: pl.semaphore_signal(
        barrier, inc=1, device_id=(z, lax.rem(e + i, NE)), device_id_type=MESH))

    lane, sub = iota((ROWS, 128), 1), iota((ROWS, 128), 0)
    eye = iota((ROWS, ROWS), 1) == iota((ROWS, ROWS), 0)
    need(decay_ref, ids_ref)
    ids_col = jnp.sum(jnp.where(eye, ids_ref[...].astype(F32), 0.0), axis=1, keepdims=True)
    near = lax.rem(lane, ROWS)
    ids_row = jnp.sum(jnp.where(sub == near, ids_col, 0.0), axis=0, keepdims=True)
    same = jnp.where((ids_col == ids_row) & (sub < near), 1.0, 0.0)
    slot_row = ids_row * 32.0 + jnp.sum(same, axis=0, keepdims=True)

    decay = jnp.concatenate([decay_ref[:, 128 * r:128 * r + 128] for r in range(TILES)], axis=0)
    upto = jnp.where(iota((128, 128), 0) <= iota((128, 128), 1), 1.0, 0.0)
    cum = dot(decay, upto, precision=PRECISE)
    tails = [jnp.zeros((1, 1), F32)]
    for r in range(1, TILES):
        tails.append(jnp.where(r % 4 == 0, 0.0, tails[r - 1] + cum[r - 1:r, 127:128]))
    running = cum + jnp.concatenate(tails, axis=0)
    running_col = running.T
    ends = [running[4 * b + 3:4 * b + 4, 127:128] for b in range(2)]
    total = ends[0] + ends[1]

    need(k_ref, v_ref)
    updates = []
    for b in range(2):
        rest = jnp.concatenate(
            [jnp.exp(ends[b] - running_col[:, 4 * b + r:4 * b + r + 1]) for r in range(4)], axis=0
        )
        decayed = (v_ref[BL * b:BL * b + BL, :].astype(F32) * rest).astype(BF16)
        updates.append(t_dot(k_ref[BL * b:BL * b + BL, :], decayed))
    own_state = jnp.exp(ends[1]) * updates[0] + updates[1]

    info[z] = jnp.concatenate([slot_row, jnp.broadcast_to(total, (1, 128))], axis=0)
    pieces[...] = own_state.reshape(NZ, 8, HD)
    pl.semaphore_wait(barrier, NZ - 1 + NE - 1)

    def turn(i):
        return lax.rem(z + i, NZ)

    def cp_info(i):
        return remote(info.at[z], info.at[z], s_info.at[i], r_info.at[i], turn(i), e)

    def cp_piece(i):
        return remote(pieces.at[turn(i)], gathered.at[z], s_pc.at[i], r_pc.at[i], turn(i), e)

    def cp_enter(i):
        return remote(entering.at[turn(i)], incoming.at[z], s_en.at[i], r_en.at[i], turn(i), e)

    def fetched(cp):
        drains.append(lambda: loop(1, NZ, lambda i: cp(i).wait_send()))

    for i in FAR:
        cp_piece(i).start()
        cp_info(i).start()
    fetched(cp_piece)
    fetched(cp_info)
    gathered[z] = pieces[z]

    cp_down = remote(wd_ref.at[parity], wd_ref.at[parity], s_wd, r_wd, partner, e)
    need(wd_ref)
    cp_down.start()
    drains.append(lambda: cp_down.wait())

    need(q_ref)
    triangle = iota((128, 128), 0) >= iota((128, 128), 1)

    def inside(r):
        b, i = divmod(r, 4)
        rows, span = pl.ds(128 * r, 128), pl.ds(BL * b, 128 * (i + 1))
        scores = dot_t(q_ref[rows, :], k_ref[span, :])
        col = running_col[:, r:r + 1]
        weights = []
        for j in range(i + 1):
            spread = col - running[4 * b + j:4 * b + j + 1, :]
            if j == i:
                spread = jnp.where(triangle, spread, -jnp.inf)
            weights.append((scores[:, 128 * j:128 * j + 128] * jnp.exp(spread)).astype(BF16))
        weights = jnp.concatenate(weights, axis=1) if i else weights[0]
        within[rows, :] = dot(weights, v_ref[span, :])

    for r in range(4):
        inside(r)

    loop(1, NZ, lambda i: cp_info(i).wait_recv())
    factors = jnp.exp(info[:, 1, :])
    loop(1, NZ, lambda i: cp_piece(i).wait_recv())
    carried = jnp.zeros((8, HD), F32)
    for n in range(NZ):
        entering[n] = carried
        carried = factors[n:n + 1, :] * carried + gathered[n]
    for i in FAR:
        cp_enter(i).start()
    fetched(cp_enter)
    incoming[z] = entering[z]
    for r in range(4, 8):
        inside(r)
    need(gain_ref)
    gain = gain_ref[...]
    loop(1, NZ, lambda i: cp_enter(i).wait_recv())
    first = incoming[...].reshape(HD, HD)

    for b in range(2):
        state = first if b == 0 else updates[0] + jnp.exp(ends[0]) * first
        state = state.astype(BF16)
        for i in range(4):
            r = 4 * b + i
            rows = pl.ds(128 * r, 128)
            across = dot(q_ref[rows, :], state) * jnp.exp(running_col[:, r:r + 1])
            attention = within[rows, :] + across
            scale = lax.rsqrt(jnp.mean(attention * attention, axis=1, keepdims=True) + EPSILON)
            normed[rows, :] = (attention * scale * gain).astype(BF16)

    def cp_heads(to):
        return remote(normed.at[pl.ds(pl.multiple_of(to * ROWS, ROWS), ROWS)], heads.at[e],
                      s_hd.at[to], r_hd.at[e], z, to)

    def cp_heads_from(frm):
        return remote(normed.at[pl.ds(0, ROWS)], heads.at[frm], s_hd.at[frm], r_hd.at[frm], z, frm)

    heads[e] = normed[pl.ds(pl.multiple_of(e * ROWS, ROWS), ROWS), :]

    def send_heads(p):
        to_chip = lax.rem(chip - z - p + 2 * NZ, NZ)
        for core in range(2):
            to = 2 * to_chip + core

            @pl.when(to != e)
            def _():
                cp_heads(to).start()

    loop(0, NZ, send_heads)
    drains.append(lambda: loop(1, NE, lambda i: cp_heads(lax.rem(e + i, NE)).wait_send()))

    quart = iota((1, 128), 1) // 32
    picks = []
    for g in range(4):
        row = jnp.zeros((1, 128), F32)
        for n in range(4):
            row += jnp.where(quart == n, info[4 * g + n, 0:1, :] + 2.0 * (4 * g + n), 0.0)
        picks.append(row)
    picks_row = jnp.concatenate(picks, axis=1).astype(jnp.int32)
    for t in range(8):
        place[128 * t:128 * t + 128, :] = jnp.where(
            iota((128, NZ * ROWS), 0) + 128 * t == picks_row, 1.0, 0.0
        ).astype(BF16)

    def cp_rows(to):
        return remote(hidden.at[to], zrows.at[z], s_zr.at[to], r_zr.at[z], to, e)

    def cp_rows_from(frm):
        return remote(hidden.at[frm], zrows.at[frm], s_zr.at[frm], r_zr.at[frm], frm, e)

    need(res_ref)

    def send_rows(p):
        odd = lax.rem(p, 2)
        c = lax.rem(z + HALF + (1 - odd) * (p // 2) - odd * ((p + 1) // 2), NZ)
        for core in range(2):
            @pl.when(2 * c + core != e)
            def _():
                cp_heads_from(2 * c + core).wait_recv()

        both = jnp.concatenate([heads[2 * c], heads[2 * c + 1]], axis=1).astype(F32)
        block = res_ref[:, pl.ds(pl.multiple_of(c * DS, DS), DS)].astype(F32)
        hidden[c] = (block + both).astype(BF16)

        @pl.when(c != z)
        def _():
            cp_rows(c).start()

    loop(0, NZ, send_rows)
    zrows[z] = hidden[z]
    drains.append(lambda: loop(1, NZ, lambda i: cp_rows(lax.rem(z + i, NZ)).wait_send()))
    need(wg_ref, wu_ref)
    loop(1, NZ, lambda i: cp_rows_from(lax.rem(z + i, NZ)).wait_recv())
    slots[...] = dot(place[...], zrows[...].reshape(NZ * ROWS, DS)).astype(BF16)

    def cp_slots(to):
        return remote(slots.at[pl.ds(pl.multiple_of(to * 32, 32), 32)], erows.at[e],
                      s_sl.at[to], r_sl.at[e], z, to)

    def cp_slots_from(frm):
        return remote(slots.at[pl.ds(0, 32)], erows.at[frm], s_sl.at[frm], r_sl.at[frm], z, frm)

    erows[e] = slots[pl.ds(pl.multiple_of(e * 32, 32), 32), :]

    def send_slots(p):
        turn = lax.rem(p, 2)
        ahead = turn * (HALF + 1 + p // 2) + (1 - turn) * (HALF - p // 2)
        to_chip = lax.rem(chip - z - ahead + 2 * NZ, NZ)
        for core in range(2):
            to = 2 * to_chip + core

            @pl.when(to != e)
            def _():
                cp_slots(to).start()

    loop(0, NZ, send_slots)
    drains.append(lambda: loop(1, NE, lambda i: cp_slots(lax.rem(e + i, NE)).wait_send()))

    def make_unplace():
        mine = jnp.where(parity == 0, picks_row[:, 0:8 * ROWS], picks_row[:, 8 * ROWS:])
        mine = mine - 16 * parity - 16 * (mine // 32)
        for g in range(2):
            lanes = jnp.broadcast_to(mine[:, 128 * g:128 * g + 128], (128, 128))
            diagonal = iota((128, 128), 0) == iota((128, 128), 1)
            col = jnp.sum(jnp.where(diagonal, lanes, 0), axis=1, keepdims=True)
            unplace[128 * g:128 * g + 128, :] = jnp.where(
                iota((128, NE * 16), 1) == col, 1.0, 0.0
            ).astype(BF16)

    def source(j):
        return lax.rem(j + chip, NZ)

    def columns(u):
        side, off = divmod(u * WIDE, FFE)
        return (wg_ref, wu_ref)[side][:, off:off + WIDE]

    def own(j, into):
        c = source(j)
        for core in range(2):
            @pl.when(2 * c + core != e)
            def _():
                cp_slots_from(2 * c + core).wait_recv()

        rows = erows[pl.ds(2 * c, 2)].reshape(CHUNK, DS)
        for u in range(SUBS):
            into[u] = dot(rows, columns(u)).astype(BF16)

    def cp_right(s, u):
        return remote(send_r.at[s, u], recv_r.at[s, u], s_rr.at[s, u], r_rr.at[s, u], right, e)

    def cp_left(s, u):
        return remote(send_l.at[s, u], recv_l.at[s, u], s_rl.at[s, u], r_rl.at[s, u], left, e)

    own(turn(HALF), own_r)
    for u in range(SUBS):
        box, cp = (send_r, cp_right) if u < SUBS // 2 else (send_l, cp_left)
        box[0, u] = own_r[u]
        cp(0, u).start()
    for s in range(1, HALF + 1):
        own(turn(HALF - s), own_r)
        if s < HALF:
            own(turn(HALF + s), own_l)
        if s == 2:
            finish()
        if s == 3:
            make_unplace()
        if s == HALF:
            break
        for u in range(SUBS):
            for box, mine, came, cp, first_half in (
                (send_r, own_r, recv_r, cp_right, True), (send_l, own_l, recv_l, cp_left, False),
            ):
                if s == 1 and (u < SUBS // 2) != first_half:
                    box[s, u] = mine[u]
                else:
                    cp(s - 1, u).wait_recv()
                    box[s, u] = (mine[u].astype(F32) + came[s - 1, u].astype(F32)).astype(BF16)
                cp(s, u).start()
    for u in range(SUBS):
        for s in range(HALF):
            if s or u < SUBS // 2:
                drains.append(lambda s=s, u=u: cp_right(s, u).wait_send())
            if s or u >= SUBS // 2:
                drains.append(lambda s=s, u=u: cp_left(s, u).wait_send())
    sums = []
    for u in range(SUBS):
        cp_left(HALF - 1, u).wait_recv()
        cp_right(HALF - 1, u).wait_recv()
        sums.append(own_r[u].astype(F32) + recv_l[HALF - 1, u].astype(F32) + recv_r[HALF - 1, u].astype(F32))
    for u in range(SUBS // 2):
        gate, up = sums[u], sums[u + SUBS // 2]
        active = (gate / (1.0 + jnp.exp(-gate)) * up).astype(BF16)
        for h in range(2):
            for core in range(2):
                act[h, z, 16 * core:16 * core + 16, WIDE * u:WIDE * u + WIDE] = (
                    active[32 * core + 16 * h:32 * core + 16 * h + 16]
                )

    def parent(k):
        return max(0, k - 2)

    reach = {1: HALF, -1: HALF - 1}

    def cp_act(way, k):
        p, d = parent(k), (1 - way) // 2
        to_half = 1 - parity if k == 1 else parity
        at = act.at[to_half, lax.rem(z - way * p + NZ, NZ)]
        return remote(at, at, s_ac.at[d, k], r_ac.at[d, k], lax.rem(z + way * (k - p) + NZ, NZ), e)

    def cp_act_in(way, k):
        at = act.at[parity, lax.rem(z - way * k + NZ, NZ)]
        return remote(at, at, s_ac.at[(1 - way) // 2, k], r_ac.at[(1 - way) // 2, k], left, e)

    def forward(way, k):
        for child in range(reach[way], 0, -1):
            if parent(child) == k:
                cp_act(way, child).start()
                drains.append(lambda way=way, k=child: cp_act(way, k).wait_send())

    def cp_produced(d):
        return remote(produced.at[d], fromexp.at[e], s_pr.at[d], r_pr.at[e], z, d)

    def cp_from(i):
        frm = lax.rem(e + i, NE)
        return remote(produced.at[frm], fromexp.at[frm], s_pr.at[frm], r_pr.at[frm], z, frm)

    def down(j):
        rows = act[parity, j]
        rows = jnp.concatenate([dot(rows, wd_ref[n]).astype(BF16) for n in range(2)], axis=1)
        for core in range(2):
            d = 2 * source(j) + core
            produced[d] = rows[16 * core:16 * core + 16]

            @pl.when(d != e)
            def _():
                cp_produced(d).start()

            @pl.when(d == e)
            def _():
                fromexp[e] = produced[d]

    for way in (1, -1):
        forward(way, 0)
    waiting = [z]
    for n in range(1, HALF // 2 + 1):
        for j in waiting:
            down(j)
        waiting = []
        for k in (2 * n - 1, 2 * n):
            for way in (1, -1):
                if k <= reach[way]:
                    cp_act_in(way, k).wait_recv()
                    forward(way, k)
                    waiting.append(lax.rem(z - way * k + NZ, NZ))
    for j in waiting:
        down(j)
    drains.append(lambda: loop(1, NE, lambda i: cp_from(i).wait_send()))
    loop(1, NE, lambda i: cp_from(i).wait_recv())
    back = dot(unplace[...], fromexp[...].reshape(NE * 16, 2 * DS)).astype(BF16)
    yrows[...] = back.reshape(8, ROWS, 2 * DS)

    def cp_back(i):
        return remote(yrows.at[i], yback.at[z // 2], s_yb.at[i], r_yb.at[z // 2], 8 * parity + i, e)

    def cp_back_from(i):
        return remote(yrows.at[i], yback.at[i], s_yb.at[i], r_yb.at[i], 2 * i + half, e)

    def sent_back(act_on):
        def one(n):
            i = lax.rem(z // 2 + n, 8)

            @pl.when(8 * parity + i != z)
            def _():
                act_on(i)
        loop(0, 8, one)

    sent_back(lambda i: cp_back(i).start())
    need(gw_ref)
    gw_col = jnp.sum(jnp.where(eye, gw_ref[...], 0.0), axis=1, keepdims=True)
    finish()

    def mix(n):
        i = lax.rem(z // 2 + 8 - n, 8)

        @pl.when(2 * i + half != z)
        def _():
            cp_back_from(i).wait_recv()

        @pl.when(2 * i + half == z)
        def _():
            yback[i] = yrows[lax.rem(z, 8)]

        rows = jnp.concatenate([hidden[2 * i], hidden[2 * i + 1]], axis=1).astype(F32)
        mixed = rows + gw_col * yback[i].astype(F32)
        out_ref[:, pl.ds(pl.multiple_of(i * 2 * DS, 2 * DS), 2 * DS)] = mixed.astype(BF16)

    loop(0, 8, mix)
    sent_back(lambda i: cp_back(i).wait_send())


def shards(q, k, v, log_decay, gain, residual, ids, gate_weights, w_gate, w_up, w_down):
    sem = pltpu.SemaphoreType.DMA
    pair = lambda *shape: [sem(shape), sem(shape)]
    args = (
        q, k, v, log_decay.T, gain.reshape(1, HD), residual, ids.T, gate_weights.T,
        w_gate[0], w_up[0], w_down[0],
    )
    scratch = [
        *[pltpu.VMEM(a.shape, a.dtype) for a in args[:-1]],
        pltpu.VMEM((2, FFE, DS), BF16),
        pltpu.VMEM((NZ, 2, 128), F32),
        *[pltpu.VMEM((NZ, 8, HD), F32)] * 4,
        pltpu.VMEM((SEC, HD), F32),
        pltpu.VMEM((SEC, HD), BF16),
        pltpu.VMEM((NE, ROWS, HD), BF16),
        pltpu.VMEM((NZ, ROWS, DS), BF16),
        pltpu.VMEM((NZ, ROWS, DS), BF16),
        pltpu.VMEM((NE * 32, NZ * ROWS), BF16),
        pltpu.VMEM((8 * ROWS, NE * 16), BF16),
        pltpu.VMEM((NE * 32, DS), BF16),
        pltpu.VMEM((NE, 32, DS), BF16),
        pltpu.VMEM((SUBS, CHUNK, WIDE), BF16),
        pltpu.VMEM((SUBS, CHUNK, WIDE), BF16),
        pltpu.VMEM((HALF, SUBS, CHUNK, WIDE), BF16),
        pltpu.VMEM((HALF, SUBS, CHUNK, WIDE), BF16),
        pltpu.VMEM((HALF, SUBS, CHUNK, WIDE), BF16),
        pltpu.VMEM((HALF, SUBS, CHUNK, WIDE), BF16),
        pltpu.VMEM((2, NZ, CHUNK // 2, FFE), BF16),
        *[pltpu.VMEM((NE, 16, 2 * DS), BF16)] * 2,
        *[pltpu.VMEM((8, ROWS, 2 * DS), BF16)] * 2,
        sem((len(args),)),
        pltpu.SemaphoreType.DMA, pltpu.SemaphoreType.DMA,
        *pair(NZ), *pair(NZ), *pair(NZ), *pair(NE), *pair(NZ), *pair(NE),
        *pair(HALF, SUBS), *pair(HALF, SUBS), *pair(2, HALF + 1), *pair(NE), *pair(8),
    ]
    return pl.pallas_call(
        kernel,
        out_shape=jax.ShapeDtypeStruct(residual.shape, BF16),
        in_specs=[pl.BlockSpec(memory_space=pltpu.HBM)] * len(args),
        out_specs=pl.BlockSpec(memory_space=pltpu.VMEM),
        scratch_shapes=scratch,
        name="layer_pair",
        compiler_params=pltpu.CompilerParams(
            collective_id=0, has_side_effects=True, vmem_limit_bytes=60 << 20
        ),
    )(*args)


def solution(mesh):
    return jax.shard_map(
        shards,
        mesh=mesh,
        in_specs=(
            P("ctx", "exp"),
            P("ctx", "exp"),
            P("ctx", "exp"),
            P("ctx", "exp"),
            P("exp"),
            P(("ctx", "exp"), None),
            P(("ctx", "exp"), None),
            P(("ctx", "exp"), None),
            P("exp", "ctx", None),
            P("exp", "ctx", None),
            P("exp", None, "ctx"),
        ),
        out_specs=P(("ctx", "exp"), None),
        check_vma=False,
    )
```

time: 166 us -> 146 us (0.88)
  Pallas kernels: 158 us -> 143 us
  local copies, waits for them, and re-layouts: 8.18 us -> 1.67 us
    pallas_call x1, Pallas kernels: 158 us -> 143 us  [shards(): pl.pallas_call(kernel, out_shape=jax.ShapeDtypeStruct(residual.shape, BF1...]
    unnamed x23 -> x1, local copies, waits for them, and re-layouts: 8.18 us -> 1.67 us
where the time goes in v2:
time: 146 us; the launch traced here: 145 us
  Pallas kernels  143 us (98%)
  local copies, waits for them, and re-layouts  1.67 us (1%)
    pallas_call x1, Pallas kernels, shards(): pl.pallas_call(kernel, out_shape=jax.ShapeDtypeStruct(residual.shape, BF1...  143 us

profile of v2, /device:TPU:1, one launch (start us, length us, event | category | flops | bytes accessed | tf_op | source)
XLA Modules:
  0.0 144.7 jit_solution(1742650116330382848)
XLA Ops:
  0.0 143.0 %layer_pair.1 = bf16[32,4096]{1,0:T(8,128)(2,1)} custom-call(bf16[1024,128]{1,0:T(8,128)(2,1)} %q_hbm.1, bf16[1024,128]{1,0:T(8,128)(2,1)} %k_hbm.1, bf16[1024,128]{1,0:T(8,128)(2,1)} %v_hbm.1, f32[1,1024]{1,0:T(1,128)} %bitcast.10, f32[1,128]{1,0:T(1,128)} %bitcast.11, bf16[32,4096]{1,0:T(8,128)(2,1)} %res_hbm.1, s32[1,32]{1,0:T(1,128)} %bitcast.12, ...), custom_call_target="tpu_custom_call" | custom-call | tf_op jit(solution)/shard_map/layer_pair/pallas_call | solution.py:510
  143.1 1.7 %copy.13 = bf16[32,4096]{1,0:T(8,128)(2,1)} copy(bf16[32,4096]{1,0:T(8,128)(2,1)} %layer_pair.1) | data formatting | bytes 524288

commit v3 on v2

--- a/solution.py
+++ b/solution.py
@@ -148,10 +148,13 @@
     fetched(cp_info)
     gathered[z] = pieces[z]
 
-    cp_down = remote(wd_ref.at[parity], wd_ref.at[parity], s_wd, r_wd, partner, e)
+    def cp_down(n):
+        at = wd_ref.at[parity, pl.ds(DS * n, DS)]
+        return remote(at, at, s_wd.at[n], r_wd.at[n], partner, e)
+
     need(wd_ref)
-    cp_down.start()
-    drains.append(lambda: cp_down.wait())
+    cp_down(0).start()
+    drains.append(lambda: loop(0, 3, lambda n: cp_down(n).wait()))
 
     need(q_ref)
     triangle = iota((128, 128), 0) >= iota((128, 128), 1)
@@ -184,6 +187,7 @@
         cp_enter(i).start()
     fetched(cp_enter)
     incoming[z] = entering[z]
+    cp_down(1).start()
     for r in range(4, 8):
         inside(r)
     need(gain_ref)
@@ -221,6 +225,7 @@
                 cp_heads(to).start()
 
     loop(0, NZ, send_heads)
+    cp_down(2).start()
     drains.append(lambda: loop(1, NE, lambda i: cp_heads(lax.rem(e + i, NE)).wait_send()))
 
     quart = iota((1, 128), 1) // 32
@@ -503,7 +508,7 @@
         *[pltpu.VMEM((NE, 16, 2 * DS), BF16)] * 2,
         *[pltpu.VMEM((8, ROWS, 2 * DS), BF16)] * 2,
         sem((len(args),)),
-        pltpu.SemaphoreType.DMA, pltpu.SemaphoreType.DMA,
+        *pair(3),
         *pair(NZ), *pair(NZ), *pair(NZ), *pair(NE), *pair(NZ), *pair(NE),
         *pair(HALF, SUBS), *pair(HALF, SUBS), *pair(2, HALF + 1), *pair(NE), *pair(8),
     ]
@@ -515,7 +520,7 @@
         scratch_shapes=scratch,
         name="layer_pair",
         compiler_params=pltpu.CompilerParams(
-            collective_id=0, has_side_effects=True, vmem_limit_bytes=60 << 20
+            collective_id=0, has_side_effects=True, vmem_limit_bytes=54848 << 10
         ),
     )(*args)
 

time: 146 us -> 140 us (0.959)
  Pallas kernels: 143 us -> 137 us
    pallas_call x1, Pallas kernels: 143 us -> 137 us  [shards(): pl.pallas_call(kernel, out_shape=jax.ShapeDtypeStruct(residual.shape, BF1...]
where the time goes in v3:
time: 140 us; the launch traced here: 139 us
  Pallas kernels  137 us (98%)
    pallas_call x1, Pallas kernels, shards(): pl.pallas_call(kernel, out_shape=jax.ShapeDtypeStruct(residual.shape, BF1...  137 us

profile of v3, /device:TPU:1, one launch (start us, length us, event | category | flops | bytes accessed | tf_op | source)
XLA Modules:
  0.0 138.6 jit_solution(10368595939599817716)
XLA Ops:
  0.0 0.0 copy-start
  0.0 0.0 copy-start.1
  0.0 0.0 copy-start.2
  0.0 0.0 copy-start.3
  0.0 0.7 copy-done
  0.7 0.0 copy-done.1
  0.7 0.0 copy-done.2
  0.7 0.0 copy-done.3
  0.7 137.1 %layer_pair.1 = bf16[32,4096]{1,0:T(8,128)(2,1)S(1)} custom-call(bf16[1024,128]{1,0:T(8,128)(2,1)} %q_hbm.1, bf16[1024,128]{1,0:T(8,128)(2,1)} %k_hbm.1, bf16[1024,128]{1,0:T(8,128)(2,1)} %v_hbm.1, f32[1,1024]{1,0:T(1,128)S(1)} %bitcast.7, f32[1,128]{1,0:T(1,128)S(1)} %bitcast.8, bf16[32,4096]{1,0:T(8,128)(2,1)} %res_hbm.1, s32[1,32]{1,0:T(1,128)S(1)} %bitcast.9, ...), custom_call_target="tpu_custom_call" | custom-call | tf_op jit(solution)/shard_map/layer_pair/pallas_call | solution.py:515
  137.9 0.7 copy.13
Async XLA Ops:
  0.0 0.7 copy-start
  0.0 0.7 copy-start.1
  0.0 0.7 copy-start.2
  0.0 0.7 copy-start.3

commit v4 on v3

--- a/solution.py
+++ b/solution.py
@@ -123,7 +123,7 @@
     own_state = jnp.exp(ends[1]) * updates[0] + updates[1]
 
     info[z] = jnp.concatenate([slot_row, jnp.broadcast_to(total, (1, 128))], axis=0)
-    pieces[...] = own_state.reshape(NZ, 8, HD)
+    pieces[...] = own_state.reshape(8, 16, HD).astype(BF16)
     pl.semaphore_wait(barrier, NZ - 1 + NE - 1)
 
     def turn(i):
@@ -133,10 +133,10 @@
         return remote(info.at[z], info.at[z], s_info.at[i], r_info.at[i], turn(i), e)
 
     def cp_piece(i):
-        return remote(pieces.at[turn(i)], gathered.at[z], s_pc.at[i], r_pc.at[i], turn(i), e)
+        return remote(pieces.at[lax.rem(turn(i), 8)], gathered.at[z], s_pc.at[i], r_pc.at[i], turn(i), e)
 
     def cp_enter(i):
-        return remote(entering.at[turn(i)], incoming.at[z], s_en.at[i], r_en.at[i], turn(i), e)
+        return remote(entering.at[turn(i)], incoming.at[lax.rem(z, 8)], s_en.at[i], r_en.at[i], turn(i), e)
 
     def fetched(cp):
         drains.append(lambda: loop(1, NZ, lambda i: cp(i).wait_send()))
@@ -146,7 +146,7 @@
         cp_info(i).start()
     fetched(cp_piece)
     fetched(cp_info)
-    gathered[z] = pieces[z]
+    gathered[z] = pieces[lax.rem(z, 8)]
 
     def cp_down(n):
         at = wd_ref.at[parity, pl.ds(DS * n, DS)]
@@ -154,7 +154,7 @@
 
     need(wd_ref)
     cp_down(0).start()
-    drains.append(lambda: loop(0, 3, lambda n: cp_down(n).wait()))
+    drains.append(lambda: cp_down(0).wait())
 
     need(q_ref)
     triangle = iota((128, 128), 0) >= iota((128, 128), 1)
@@ -179,21 +179,24 @@
     loop(1, NZ, lambda i: cp_info(i).wait_recv())
     factors = jnp.exp(info[:, 1, :])
     loop(1, NZ, lambda i: cp_piece(i).wait_recv())
-    carried = jnp.zeros((8, HD), F32)
+    carried = jnp.zeros((16, HD), F32)
     for n in range(NZ):
-        entering[n] = carried
-        carried = factors[n:n + 1, :] * carried + gathered[n]
-    for i in FAR:
+        entering[n] = carried.astype(BF16)
+        carried = factors[n:n + 1, :] * carried + gathered[n].astype(F32)
+    around = (12, 13, 3, 14, 2, 15, 1)
+    for i in around:
         cp_enter(i).start()
-    fetched(cp_enter)
-    incoming[z] = entering[z]
+        drains.append(lambda i=i: cp_enter(i).wait_send())
+    incoming[lax.rem(z, 8)] = entering[z]
     cp_down(1).start()
+    drains.append(lambda: cp_down(1).wait())
     for r in range(4, 8):
         inside(r)
     need(gain_ref)
     gain = gain_ref[...]
-    loop(1, NZ, lambda i: cp_enter(i).wait_recv())
-    first = incoming[...].reshape(HD, HD)
+    for i in around:
+        cp_enter(i).wait_recv()
+    first = incoming[...].reshape(HD, HD).astype(F32)
 
     for b in range(2):
         state = first if b == 0 else updates[0] + jnp.exp(ends[0]) * first
@@ -226,6 +229,7 @@
 
     loop(0, NZ, send_heads)
     cp_down(2).start()
+    drains.append(lambda: cp_down(2).wait())
     drains.append(lambda: loop(1, NE, lambda i: cp_heads(lax.rem(e + i, NE)).wait_send()))
 
     quart = iota((1, 128), 1) // 32
@@ -310,8 +314,8 @@
         return lax.rem(j + chip, NZ)
 
     def columns(u):
-        side, off = divmod(u * WIDE, FFE)
-        return (wg_ref, wu_ref)[side][:, off:off + WIDE]
+        off = u // 2 * WIDE
+        return (wg_ref, wu_ref)[u % 2][:, off:off + WIDE]
 
     def own(j, into):
         c = source(j)
@@ -361,40 +365,42 @@
                 drains.append(lambda s=s, u=u: cp_right(s, u).wait_send())
             if s or u >= SUBS // 2:
                 drains.append(lambda s=s, u=u: cp_left(s, u).wait_send())
-    sums = []
-    for u in range(SUBS):
-        cp_left(HALF - 1, u).wait_recv()
-        cp_right(HALF - 1, u).wait_recv()
-        sums.append(own_r[u].astype(F32) + recv_l[HALF - 1, u].astype(F32) + recv_r[HALF - 1, u].astype(F32))
-    for u in range(SUBS // 2):
-        gate, up = sums[u], sums[u + SUBS // 2]
+    def parent(k):
+        return max(0, k - 2)
+
+    def reach(v, way):
+        return HALF if way > 0 else HALF - 1
+
+    def cp_act(v, way, k):
+        p, d = parent(k), (1 - way) // 2
+        to_half = 1 - parity if k == 1 else parity
+        at = act.at[v, to_half, lax.rem(z - way * p + NZ, NZ)]
+        return remote(at, at, s_ac.at[v, d, k], r_ac.at[v, d, k], lax.rem(z + way * (k - p) + NZ, NZ), e)
+
+    def cp_act_in(v, way, k):
+        d = (1 - way) // 2
+        at = act.at[v, parity, lax.rem(z - way * k + NZ, NZ)]
+        return remote(at, at, s_ac.at[v, d, k], r_ac.at[v, d, k], left, e)
+
+    def forward(v, way, k):
+        for child in range(reach(v, way), 0, -1):
+            if parent(child) == k:
+                cp_act(v, way, child).start()
+                drains.append(lambda k=child: cp_act(v, way, k).wait_send())
+
+    for v in range(SUBS // 2):
+        sums = []
+        for u in (2 * v, 2 * v + 1):
+            cp_left(HALF - 1, u).wait_recv()
+            cp_right(HALF - 1, u).wait_recv()
+            sums.append(own_r[u].astype(F32) + recv_l[HALF - 1, u].astype(F32) + recv_r[HALF - 1, u].astype(F32))
+        gate, up = sums
         active = (gate / (1.0 + jnp.exp(-gate)) * up).astype(BF16)
         for h in range(2):
             for core in range(2):
-                act[h, z, 16 * core:16 * core + 16, WIDE * u:WIDE * u + WIDE] = (
-                    active[32 * core + 16 * h:32 * core + 16 * h + 16]
-                )
-
-    def parent(k):
-        return max(0, k - 2)
-
-    reach = {1: HALF, -1: HALF - 1}
-
-    def cp_act(way, k):
-        p, d = parent(k), (1 - way) // 2
-        to_half = 1 - parity if k == 1 else parity
-        at = act.at[to_half, lax.rem(z - way * p + NZ, NZ)]
-        return remote(at, at, s_ac.at[d, k], r_ac.at[d, k], lax.rem(z + way * (k - p) + NZ, NZ), e)
-
-    def cp_act_in(way, k):
-        at = act.at[parity, lax.rem(z - way * k + NZ, NZ)]
-        return remote(at, at, s_ac.at[(1 - way) // 2, k], r_ac.at[(1 - way) // 2, k], left, e)
-
-    def forward(way, k):
-        for child in range(reach[way], 0, -1):
-            if parent(child) == k:
-                cp_act(way, child).start()
-                drains.append(lambda way=way, k=child: cp_act(way, k).wait_send())
+                act[v, h, z, 16 * core:16 * core + 16] = active[32 * core + 16 * h:32 * core + 16 * h + 16]
+        for way in (1, -1):
+            forward(v, way, 0)
 
     def cp_produced(d):
         return remote(produced.at[d], fromexp.at[e], s_pr.at[d], r_pr.at[e], z, d)
@@ -404,7 +410,7 @@
         return remote(produced.at[frm], fromexp.at[frm], s_pr.at[frm], r_pr.at[frm], z, frm)
 
     def down(j):
-        rows = act[parity, j]
+        rows = jnp.concatenate([act[v, parity, j] for v in range(SUBS // 2)], axis=1)
         rows = jnp.concatenate([dot(rows, wd_ref[n]).astype(BF16) for n in range(2)], axis=1)
         for core in range(2):
             d = 2 * source(j) + core
@@ -418,19 +424,19 @@
             def _():
                 fromexp[e] = produced[d]
 
-    for way in (1, -1):
-        forward(way, 0)
     waiting = [z]
     for n in range(1, HALF // 2 + 1):
         for j in waiting:
             down(j)
         waiting = []
-        for k in (2 * n - 1, 2 * n):
-            for way in (1, -1):
-                if k <= reach[way]:
-                    cp_act_in(way, k).wait_recv()
-                    forward(way, k)
-                    waiting.append(lax.rem(z - way * k + NZ, NZ))
+        for v in range(SUBS // 2):
+            for k in (2 * n - 1, 2 * n):
+                for way in (1, -1):
+                    if k <= reach(v, way):
+                        cp_act_in(v, way, k).wait_recv()
+                        forward(v, way, k)
+                        if v:
+                            waiting.append(lax.rem(z - way * k + NZ, NZ))
     for j in waiting:
         down(j)
     drains.append(lambda: loop(1, NE, lambda i: cp_from(i).wait_send()))
@@ -446,7 +452,10 @@
 
     def sent_back(act_on):
         def one(n):
-            i = lax.rem(z // 2 + n, 8)
+            odd = lax.rem(n, 2)
+            step = odd * ((n + 1) // 2) + (1 - odd) * (8 - n // 2)
+            near = jnp.where(half == parity, 12 - step, step)
+            i = lax.rem(z + near, 8)
 
             @pl.when(8 * parity + i != z)
             def _():
@@ -488,7 +497,10 @@
         *[pltpu.VMEM(a.shape, a.dtype) for a in args[:-1]],
         pltpu.VMEM((2, FFE, DS), BF16),
         pltpu.VMEM((NZ, 2, 128), F32),
-        *[pltpu.VMEM((NZ, 8, HD), F32)] * 4,
+        pltpu.VMEM((8, 16, HD), BF16),
+        pltpu.VMEM((NZ, 16, HD), BF16),
+        pltpu.VMEM((NZ, 16, HD), BF16),
+        pltpu.VMEM((8, 16, HD), BF16),
         pltpu.VMEM((SEC, HD), F32),
         pltpu.VMEM((SEC, HD), BF16),
         pltpu.VMEM((NE, ROWS, HD), BF16),
@@ -504,13 +516,13 @@
         pltpu.VMEM((HALF, SUBS, CHUNK, WIDE), BF16),
         pltpu.VMEM((HALF, SUBS, CHUNK, WIDE), BF16),
         pltpu.VMEM((HALF, SUBS, CHUNK, WIDE), BF16),
-        pltpu.VMEM((2, NZ, CHUNK // 2, FFE), BF16),
+        pltpu.VMEM((SUBS // 2, 2, NZ, CHUNK // 2, WIDE), BF16),
         *[pltpu.VMEM((NE, 16, 2 * DS), BF16)] * 2,
         *[pltpu.VMEM((8, ROWS, 2 * DS), BF16)] * 2,
         sem((len(args),)),
         *pair(3),
         *pair(NZ), *pair(NZ), *pair(NZ), *pair(NE), *pair(NZ), *pair(NE),
-        *pair(HALF, SUBS), *pair(HALF, SUBS), *pair(2, HALF + 1), *pair(NE), *pair(8),
+        *pair(HALF, SUBS), *pair(HALF, SUBS), *pair(SUBS // 2, 2, HALF + 1), *pair(NE), *pair(8),
     ]
     return pl.pallas_call(
         kernel,

time: 140 us -> 137 us (0.979)
  Pallas kernels: 137 us -> 135 us
    pallas_call x1, Pallas kernels: 137 us -> 135 us  [shards(): pl.pallas_call(kernel, out_shape=jax.ShapeDtypeStruct(residual.shape, BF1...]
where the time goes in v4:
time: 137 us; the launch traced here: 136 us
  Pallas kernels  135 us (99%)
  local copies, waits for them, and re-layouts  1.39 us (1%)
    pallas_call x1, Pallas kernels, shards(): pl.pallas_call(kernel, out_shape=jax.ShapeDtypeStruct(residual.shape, BF1...  135 us

profile of v4, /device:TPU:1, one launch (start us, length us, event | category | flops | bytes accessed | tf_op | source)
XLA Modules:
  0.0 136.3 jit_solution(12752693138712414289)
XLA Ops:
  0.0 0.0 copy-start
  0.0 0.0 copy-start.1
  0.0 0.0 copy-start.2
  0.0 0.0 copy-start.3
  0.0 0.7 copy-done
  0.7 0.0 copy-done.1
  0.7 0.0 copy-done.2
  0.7 0.0 copy-done.3
  0.7 134.9 %layer_pair.1 = bf16[32,4096]{1,0:T(8,128)(2,1)S(1)} custom-call(bf16[1024,128]{1,0:T(8,128)(2,1)} %q_hbm.1, bf16[1024,128]{1,0:T(8,128)(2,1)} %k_hbm.1, bf16[1024,128]{1,0:T(8,128)(2,1)} %v_hbm.1, f32[1,1024]{1,0:T(1,128)S(1)} %bitcast.7, f32[1,128]{1,0:T(1,128)S(1)} %bitcast.8, bf16[32,4096]{1,0:T(8,128)(2,1)} %res_hbm.1, s32[1,32]{1,0:T(1,128)S(1)} %bitcast.9, ...), custom_call_target="tpu_custom_call" | custom-call | tf_op jit(solution)/shard_map/layer_pair/pallas_call | solution.py:527
  135.6 0.7 copy.13
Async XLA Ops:
  0.0 0.7 copy-start
  0.0 0.7 copy-start.1
  0.0 0.7 copy-start.2
  0.0 0.7 copy-start.3

commit v5 on v4

--- a/solution.py
+++ b/solution.py
@@ -455,7 +455,7 @@
             odd = lax.rem(n, 2)
             step = odd * ((n + 1) // 2) + (1 - odd) * (8 - n // 2)
             near = jnp.where(half == parity, 12 - step, step)
-            i = lax.rem(z + near, 8)
+            i = lax.rem(z // 2 + n, 8)
 
             @pl.when(8 * parity + i != z)
             def _():

time: 137 us -> 136 us (level)
  the two profiles are of different devices: /device:TPU:1 before, /device:TPU:69 now
where the time goes in v5:
time: 136 us
  Pallas kernels  135 us (99%)
  local copies, waits for them, and re-layouts  1.39 us (1%)
    pallas_call x1, Pallas kernels, shards(): pl.pallas_call(kernel, out_shape=jax.ShapeDtypeStruct(residual.shape, BF1...  135 us

profile of v5, /device:TPU:69, one launch (start us, length us, event | category | flops | bytes accessed | tf_op | source)
XLA Modules:
  0.0 136.0 jit_solution(1027553815030572724)
XLA Ops:
  0.0 0.0 copy-start
  0.0 0.0 copy-start.1
  0.0 0.0 copy-start.2
  0.0 0.0 copy-start.3
  0.0 0.7 copy-done
  0.7 0.0 copy-done.1
  0.7 0.0 copy-done.2
  0.7 0.0 copy-done.3
  0.7 134.6 %layer_pair.1 = bf16[32,4096]{1,0:T(8,128)(2,1)S(1)} custom-call(bf16[1024,128]{1,0:T(8,128)(2,1)} %q_hbm.1, bf16[1024,128]{1,0:T(8,128)(2,1)} %k_hbm.1, bf16[1024,128]{1,0:T(8,128)(2,1)} %v_hbm.1, f32[1,1024]{1,0:T(1,128)S(1)} %bitcast.7, f32[1,128]{1,0:T(1,128)S(1)} %bitcast.8, bf16[32,4096]{1,0:T(8,128)(2,1)} %res_hbm.1, s32[1,32]{1,0:T(1,128)S(1)} %bitcast.9, ...), custom_call_target="tpu_custom_call" | custom-call | tf_op jit(solution)/shard_map/layer_pair/pallas_call | solution.py:527
  135.3 0.7 copy.13
Async XLA Ops:
  0.0 0.7 copy-start
  0.0 0.7 copy-start.1
  0.0 0.7 copy-start.2
  0.0 0.7 copy-start.3
